TPU v7x, 256 devices: a whole 4x4x8 slice. The times are simulated.
256 devices in a mesh: tm: 32 (over z_lo, x, core), mode: 8 (over z_hi, y).
Axes of the slice: x: 4, y: 4, z: 8 (z_hi: 2, z_lo: 4; z = z_hi * 4 + z_lo), core: 2. Of those that a mesh axis runs over, the one named last changes fastest.
Arguments:
- fields: float32 [32, 2, 1024, 1024], P('tm', None, 'mode'), may hold values from -2.5 to 2.5
- offsets: int32 [32, 2], P('tm'), may hold values from 1 to 4
Outputs:
- products: float32 [32, 2, 2, 1024, 1024], P('tm', None, None, 'mode')
- correlators: float32 [32, 2], P('tm')
All inputs are finite; a program needn't handle non-finite values.
Results may differ from a plain program's by a relative error of at most 0.0003.
Values sent between devices are 32-bit elements; how exact they have to be, the bound alone decides.
A program may use at most 128 MiB of HBM per device.

v0:
```python
import jax
import jax.numpy as jnp
from jax import lax
from jax.sharding import PartitionSpec as P


def passed_along(block, axis, distance):
    devices = range(lax.axis_size(axis))
    route = [((i - distance) % len(devices), i) for i in devices]
    return lax.ppermute(block, axis, route)


def body(fields, offsets):
    hi = lax.Precision.HIGHEST
    own = fields[0]
    pairs = offsets.shape[1]
    width = own.shape[2]
    candidates = []
    for reach_step in range(1, 5):
        candidates.append(passed_along(fields, "tm", -reach_step))
    chosen = []
    for pair_index in range(pairs):
        picked = jnp.zeros_like(own)
        for reach_step in range(1, 5):
            picked = jnp.where(
                offsets[0, pair_index] == reach_step, candidates[reach_step - 1][0], picked
            )
        chosen.append(picked)
    sinks = jnp.stack(chosen)
    piece = lax.all_gather(sinks, "mode", axis=2, tiled=True)
    left_re = own[0]
    left_im = own[1]
    real = jnp.einsum("rc,kcn->krn", left_re, piece[:, 0], precision=hi) - jnp.einsum(
        "rc,kcn->krn", left_im, piece[:, 1], precision=hi
    )
    imag = jnp.einsum("rc,kcn->krn", left_re, piece[:, 1], precision=hi) + jnp.einsum(
        "rc,kcn->krn", left_im, piece[:, 0], precision=hi
    )
    forward = jnp.stack([real, imag], axis=1)
    piece = lax.all_gather(own, "mode", axis=1, tiled=True)
    left_re = sinks[:, 0]
    left_im = sinks[:, 1]
    real = jnp.einsum("krc,cn->krn", left_re, piece[0], precision=hi) - jnp.einsum(
        "krc,cn->krn", left_im, piece[1], precision=hi
    )
    imag = jnp.einsum("krc,cn->krn", left_re, piece[1], precision=hi) + jnp.einsum(
        "krc,cn->krn", left_im, piece[0], precision=hi
    )
    partner = jnp.stack([real, imag], axis=1)
    partial_trace = jnp.sum(forward * partner, axis=(1, 2, 3)) / jnp.float32(width)
    traces = lax.psum(partial_trace, "mode")
    return (forward[None], traces[None])


def solution(mesh):
    in_specs = (P("tm", None, "mode", None), P("tm", None))
    out_specs = (P("tm", None, None, "mode", None), P("tm", None))
    return jax.shard_map(body, mesh=mesh, in_specs=in_specs, out_specs=out_specs, check_vma=False)
```

profile of v0, /device:TPU:7, one launch (start us, length us, event | category | flops | bytes accessed | tf_op | source)
XLA Modules:
  0.0 625.9 jit_solution(7827979714371582979)
XLA Ops:
  7.2 0.0 all-gather.6.cloned.1.call-start
  7.2 0.7 all-gather.6.cloned.1.call-update
  7.9 0.0 all-gather.4.cloned.1.call-start
  7.9 1.6 copy.4
  9.5 0.8 collective-permute-start.3
  10.3 0.6 collective-permute-start.2
  10.8 0.5 collective-permute-start.1
  11.3 7.3 %collective-permute-start = (f32[1,2,128,1024]{2,3,0,1:T(8,128)S(1)}, f32[1,2,128,1024]{2,3,0,1:T(8,128)S(1)}, u32[]{:S(2)}, u32[]{:S(2)}) collective-permute-start(f32[1,2,128,1024]{2,3,0,1:T(8,128)S(1)} %copy.4), channel_id=1, source_target_pairs={{32,0},{40,8},{48,16},{56,24},{64,32},{72,40},{80,48},{88,56},{96,... | collective-permute-start | bytes 3145736 | tf_op jit(solution)/shard_map/ppermute | solution.py:10
  18.6 1.3 fusion.38
  25.1 43.7 %collective-permute-done.3 = f32[1,2,128,1024]{2,3,0,1:T(8,128)S(1)} collective-permute-done((f32[1,2,128,1024]{2,3,0,1:T(8,128)S(1)}, f32[1,2,128,1024]{2,3,0,1:T(8,128)S(1)}, u32[]{:S(2)}, u32[]{:S(2)}) %collective-permute-start.3) | collective-permute-done | bytes 1048608 | tf_op jit(solution)/shard_map/ppermute | solution.py:10
  68.8 0.5 collective-permute-done.2
  69.3 0.0 collective-permute-done.1
  69.3 9.4 %collective-permute-done = f32[1,2,128,1024]{2,3,0,1:T(8,128)S(1)} collective-permute-done((f32[1,2,128,1024]{2,3,0,1:T(8,128)S(1)}, f32[1,2,128,1024]{2,3,0,1:T(8,128)S(1)}, u32[]{:S(2)}, u32[]{:S(2)}) %collective-permute-start) | collective-permute-done | bytes 1048608 | tf_op jit(solution)/shard_map/ppermute | solution.py:10
  78.7 0.3 select_select_fusion.1
  79.0 1.5 pad_maximum_fusion
  80.5 0.0 all-gather.4.cloned.1.call-update
  80.5 117.2 %all-gather.6.cloned.1.call-done = f32[1,2,1024,1024]{3,2,1,0:T(8,128)} async-done(((f32[1,2,128,1024]{3,2,1,0:T(8,128)}), f32[1,2,1024,1024]{3,2,1,0:T(8,128)}) %all-gather.6.cloned.1.call-update) | async-done | bytes 8388624 | tf_op jit(solution)/shard_map/all_gather | solution.py:40
  197.7 0.0 slice-start
  197.7 9.2 %fusion.4 = f32[2,128,1024]{1,2,0:T(8,128)S(1)} fusion(f32[1,2,1024,1024]{3,2,1,0:T(8,128)} %all-gather.6.cloned.1.call-done, f32[1,2,128,1024]{2,3,0,1:T(8,128)S(1)} %get-tuple-element.4, f32[1,2,128,1024]{2,3,0,1:T(8,128)S(1)} %get-tuple-element.5), kind=kOutput, calls=%fused_computation.8 | convolution fusion | flops 3221487616 | bytes 7340032 | tf_op jit(solution)/shard_map/krc,cn->krn/dot_general | solution.py:46
  206.9 0.0 slice-start.1
  206.9 10.1 %fusion.11 = f32[2,1,128,1024]{2,3,0,1:T(8,128)} fusion(f32[2,128,1024]{1,2,0:T(8,128)S(1)} %fusion.4, f32[1,2,1024,1024]{3,2,1,0:T(8,128)} %all-gather.6.cloned.1.call-done, f32[1,2,128,1024]{2,3,0,1:T(8,128)S(1)} %get-tuple-element.4, f32[1,2,128,1024]{2,3,0,1:T(8,128)S(1)} %get-tuple-element.5), kind=kOutput, calls=%fused_computation.22 | convolution fusion | flops 3221749760 | bytes 8388608 | tf_op jit(solution)/shard_map/krc,cn->krn/dot_general | solution.py:46
  217.1 0.0 slice-done
  217.1 0.0 slice-done.1
  217.1 7.0 %fusion.7 = f32[2,128,1024]{1,2,0:T(8,128)S(1)} fusion(f32[1,2,1024,1024]{3,2,1,0:T(8,128)S(1)} %bitcast.83, f32[1,2,128,1024]{2,3,0,1:T(8,128)S(1)} %get-tuple-element.4, f32[1,2,128,1024]{2,3,0,1:T(8,128)S(1)} %get-tuple-element.5), kind=kOutput, calls=%fused_computation.11 | convolution fusion | flops 3221487616 | bytes 7340032 | tf_op jit(solution)/shard_map/krc,cn->krn/dot_general | solution.py:43
  224.1 0.0 copy-start.1
  224.1 7.9 %fusion.13 = f32[2,1,128,1024]{2,3,0,1:T(8,128)} fusion(f32[2,128,1024]{1,2,0:T(8,128)S(1)} %fusion.7, f32[1,2,1024,1024]{3,2,1,0:T(8,128)S(1)} %bitcast.83, f32[1,2,128,1024]{2,3,0,1:T(8,128)S(1)} %get-tuple-element.4, f32[1,2,128,1024]{2,3,0,1:T(8,128)S(1)} %get-tuple-element.5), kind=kOutput, calls=%fused_computation.24 | convolution fusion | flops 3221749760 | bytes 8388608 | tf_op jit(solution)/shard_map/krc,cn->krn/dot_general | solution.py:43
  232.0 328.5 %all-gather.4.cloned.1.call-done = f32[2,2,1024,1024]{2,3,0,1:T(8,128)} async-done(((f32[2,2,128,1024]{2,3,0,1:T(8,128)}), f32[2,2,1024,1024]{2,3,0,1:T(8,128)}) %all-gather.4.cloned.1.call-update) | async-done | bytes 16777232 | tf_op jit(solution)/shard_map/all_gather | solution.py:30
  560.5 0.0 copy-done.1
  560.5 0.0 copy-start
  560.5 9.2 %fusion = f32[2,1024,128]{2,1,0:T(8,128)S(1)} fusion(f32[2,2,1024,1024]{2,3,0,1:T(8,128)} %all-gather.4.cloned.1.call-done, f32[1,2,128,1024]{3,2,1,0:T(8,128)S(1)} %copy-done.1), kind=kOutput, calls=%fused_computation.2 | convolution fusion | flops 3221225472 | bytes 9961472 | tf_op jit(solution)/shard_map/rc,kcn->krn/dot_general | solution.py:36
  569.7 9.3 %fusion.3 = f32[2,1024,128]{2,1,0:T(8,128)S(1)} fusion(f32[2,2,1024,1024]{2,3,0,1:T(8,128)} %all-gather.4.cloned.1.call-done, f32[1,2,128,1024]{3,2,1,0:T(8,128)S(1)} %copy-done.1), kind=kOutput, calls=%fused_computation.5 | convolution fusion | flops 3221225472 | bytes 9961472 | tf_op jit(solution)/shard_map/rc,kcn->krn/dot_general | solution.py:33
  579.0 0.0 copy-done
  579.0 7.0 %fusion.15 = f32[2,1,128,1024]{2,3,0,1:T(8,128)S(1)} fusion(f32[2,1024,128]{2,1,0:T(8,128)S(1)} %fusion, f32[2,2,1024,1024]{2,3,0,1:T(8,128)S(1)} %copy-done, f32[1,2,128,1024]{3,2,1,0:T(8,128)S(1)} %copy-done.1), kind=kOutput, calls=%fused_computation.26 | convolution fusion | flops 3221487616 | bytes 11010048 | tf_op jit(solution)/shard_map/rc,kcn->krn/dot_general | solution.py:36
  586.0 0.0 copy-start.2
  586.1 0.0 copy-start.3
  586.1 7.3 %fusion.17 = f32[2,1,128,1024]{2,3,0,1:T(8,128)S(1)} fusion(f32[2,1024,128]{2,1,0:T(8,128)S(1)} %fusion.3, f32[2,2,1024,1024]{2,3,0,1:T(8,128)S(1)} %copy-done, f32[1,2,128,1024]{3,2,1,0:T(8,128)S(1)} %copy-done.1), kind=kOutput, calls=%fused_computation.28 | convolution fusion | flops 3221487616 | bytes 11010048 | tf_op jit(solution)/shard_map/rc,kcn->krn/dot_general | solution.py:33
  593.4 0.0 copy-done.2
  593.4 0.0 copy-done.3
  593.4 0.4 fusion.8
  593.8 23.0 %psum.7 = f32[1,2]{1,0:T(1,128)} all-reduce(f32[1,2]{1,0:T(1,128)S(1)} %multiply_bitcast_fusion), channel_id=1, replica_groups=mesh['tm'=32,'mode'=8] {'mode'}, use_global_device_ids=true, to_apply=%region_1.2 | all-reduce | flops 2 | bytes 16 | tf_op jit(solution)/shard_map/psum | solution.py:51
  616.8 1.8 copy.16
  (2 shorter events, 0.0 us)
Async XLA Ops:
  7.2 190.6 %all-gather.6.cloned.1.call-start = ((), (), s32[]{:S(2)}) async-start(), calls=%async_computation.1 | async-start | bytes 9437184 | tf_op jit(solution)/shard_map/all_gather | solution.py:40
  7.9 552.6 %all-gather.4.cloned.1.call-start = ((), (), s32[]{:S(2)}) async-start(), calls=%async_computation | async-start | bytes 18874368 | tf_op jit(solution)/shard_map/all_gather | solution.py:30
  9.5 59.3 %collective-permute-start.3 = (f32[1,2,128,1024]{2,3,0,1:T(8,128)S(1)}, f32[1,2,128,1024]{2,3,0,1:T(8,128)S(1)}, u32[]{:S(2)}, u32[]{:S(2)}) collective-permute-start(f32[1,2,128,1024]{2,3,0,1:T(8,128)S(1)} %copy.4), channel_id=1, source_target_pairs={{8,0},{16,8},{24,16},{32,24},{40,32},{48,40},{56,48},{64,56},{72,6... | collective-permute-start | bytes 3145736 | tf_op jit(solution)/shard_map/ppermute | solution.py:10
  10.3 59.1 %collective-permute-start.2 = (f32[1,2,128,1024]{2,3,0,1:T(8,128)S(1)}, f32[1,2,128,1024]{2,3,0,1:T(8,128)S(1)}, u32[]{:S(2)}, u32[]{:S(2)}) collective-permute-start(f32[1,2,128,1024]{2,3,0,1:T(8,128)S(1)} %copy.4), channel_id=1, source_target_pairs={{16,0},{24,8},{32,16},{40,24},{48,32},{56,40},{64,48},{72,56},{80,... | collective-permute-start | bytes 3145736 | tf_op jit(solution)/shard_map/ppermute | solution.py:10
  10.8 58.5 %collective-permute-start.1 = (f32[1,2,128,1024]{2,3,0,1:T(8,128)S(1)}, f32[1,2,128,1024]{2,3,0,1:T(8,128)S(1)}, u32[]{:S(2)}, u32[]{:S(2)}) collective-permute-start(f32[1,2,128,1024]{2,3,0,1:T(8,128)S(1)} %copy.4), channel_id=1, source_target_pairs={{24,0},{32,8},{40,16},{48,24},{56,32},{64,40},{72,48},{80,56},{88,... | collective-permute-start | bytes 3145736 | tf_op jit(solution)/shard_map/ppermute | solution.py:10
  11.3 67.4 %collective-permute-start = (f32[1,2,128,1024]{2,3,0,1:T(8,128)S(1)}, f32[1,2,128,1024]{2,3,0,1:T(8,128)S(1)}, u32[]{:S(2)}, u32[]{:S(2)}) collective-permute-start(f32[1,2,128,1024]{2,3,0,1:T(8,128)S(1)} %copy.4), channel_id=1, source_target_pairs={{32,0},{40,8},{48,16},{56,24},{64,32},{72,40},{80,48},{88,56},{96,... | collective-permute-start | bytes 3145736 | tf_op jit(solution)/shard_map/ppermute | solution.py:10
  197.7 19.3 %slice-start = ((s8[8388608]{0:T(1024)(128)(4,1)}), s8[4194304]{0:T(1024)(128)(4,1)S(1)}, s32[]{:S(2)}) async-start(s8[8388608]{0:T(1024)(128)(4,1)} %bitcast.82), calls=%async_computation.2 | async-start | bytes 8388608
  206.9 10.1 %slice-start.1 = ((s8[8388608]{0:T(1024)(128)(4,1)}), s8[4194304]{0:T(1024)(128)(4,1)S(1)}, s32[]{:S(2)}) async-start(s8[8388608]{0:T(1024)(128)(4,1)} %bitcast.82), calls=%async_computation.3 | async-start | bytes 8388608
  224.1 336.4 %copy-start.1 = (f32[1,2,128,1024]{3,2,1,0:T(8,128)S(1)}, f32[1,2,128,1024]{3,2,1,0:T(8,128)}, u32[]{:S(2)}) copy-start(f32[1,2,128,1024]{3,2,1,0:T(8,128)} %param.2) | copy-start | bytes 3145732
  560.5 18.5 %copy-start = (f32[2,2,1024,1024]{2,3,0,1:T(8,128)S(1)}, f32[2,2,1024,1024]{2,3,0,1:T(8,128)}, u32[]{:S(2)}) copy-start(f32[2,2,1024,1024]{2,3,0,1:T(8,128)} %all-gather.4.cloned.1.call-done) | copy-start | bytes 50331652
  586.0 7.3 %copy-start.2 = (f32[2,1,128,1024]{2,3,0,1:T(8,128)S(1)}, f32[2,1,128,1024]{2,3,0,1:T(8,128)}, u32[]{:S(2)}) copy-start(f32[2,1,128,1024]{2,3,0,1:T(8,128)} %fusion.11) | copy-start | bytes 3145732
  586.1 7.3 %copy-start.3 = (f32[2,1,128,1024]{2,3,0,1:T(8,128)S(1)}, f32[2,1,128,1024]{2,3,0,1:T(8,128)}, u32[]{:S(2)}) copy-start(f32[2,1,128,1024]{2,3,0,1:T(8,128)} %fusion.13) | copy-start | bytes 3145732
Sparse Core Ops, SparseCore 0:
  10.6 187.0 all-gather.5
  200.8 359.6 all-gather.3
where the time goes:
time: 636 us; the launch traced here: 626 us
  waiting for transfers between devices  500 us (79%)
  matrix products  67.1 us (11%)
  blocking collectives  23 us (4%)
  between operations  19.8 us (3%)
  starting transfers between devices  9.18 us (1%)
    all_gather x1, waiting for transfers between devices, body(): piece = lax.all_gather(sinks, 'mode', axis=2, tiled=True)  328 us
    all_gather x1, waiting for transfers between devices, body(): piece = lax.all_gather(own, 'mode', axis=1, tiled=True)  117 us
    ppermute x4, waiting for transfers between devices, passed_along(): return lax.ppermute(block, axis, route)  53.6 us
    psum x1, blocking collectives, body(): traces = lax.psum(partial_trace, 'mode')  23 us
  transfers between devices with their start and end apart: 6, of which 5 were waited for; matrix products, arithmetic and copies ran while one was open for 6% of the time, Pallas kernels for 0%

commit v1 on v0

v1 whole, which is shorter than its diff:
```python
import functools

import jax
import jax.numpy as jnp
from jax import lax
from jax.experimental import pallas as pl
from jax.experimental.pallas import tpu as pltpu
from jax.sharding import PartitionSpec as P

MESH = pl.DeviceIdType.MESH
F32 = jnp.float32
BF16 = jnp.bfloat16
NX, NY, NZ = 4, 4, 4


def split(value):
    hi = value.astype(BF16)
    lo = (value - hi.astype(F32)).astype(BF16)
    return hi, lo


def kernel(rows, own, offs, out, corr, g, of, tsel, sl, tl, sb, tb, ls, lt, rs, rt, pacc, qacc, part, parts,
           ssem, rsem, psem, trsem, lsem):
    half = 4 * rows
    tm = lax.axis_index("tm")
    mode = lax.axis_index("mode")
    a = tm % 2
    x = (tm // 2) % NX
    zl = tm // (2 * NX)
    y = mode % NY
    h = mode // NY

    def dev(core=a, xx=x, zz=zl, yy=y, hh=h):
        return ((zz * NX + xx) * 2 + core, hh * NY + yy)

    def step(v, d, n=4):
        return (v + d + n) % n

    sib = dev(core=1 - a)

    bar = pltpu.get_barrier_semaphore()
    count = 0
    for dc in range(2):
        for dh in range(2):
            for dy in range(4):
                if dc or dh or dy:
                    pl.semaphore_signal(bar, 1, device_id=dev(core=(a + dc) % 2, yy=step(y, dy), hh=(h + dh) % 2), device_id_type=MESH)
                    count += 1
    for d in (1, 2, 3):
        pl.semaphore_signal(bar, 1, device_id=dev(xx=step(x, d)), device_id_type=MESH)
        count += 1
    for d in (1, 3):
        pl.semaphore_signal(bar, 1, device_id=dev(zz=step(zl, d)), device_id_type=MESH)
        count += 1
    for k in range(2):
        of[a, k] = jnp.full(of.shape[2:], offs[0, k].astype(F32), F32)
    pl.semaphore_wait(bar, count)

    sends = []
    counter = [0]

    def remote(src, dst, device, start=True, when=None, rsem_at=None):
        i = counter[0]
        counter[0] += 1
        cp = pltpu.make_async_remote_copy(
            src_ref=src, dst_ref=dst, send_sem=ssem.at[i], recv_sem=rsem.at[i] if rsem_at is None else rsem_at,
            device_id=device, device_id_type=MESH)
        if when is None:
            cp.start()
        else:
            pl.when(when)(cp.start)
        sends.append((cp, when))
        return cp

    def local(src, dst, i):
        cp = pltpu.make_async_copy(src, dst, lsem.at[i])
        cp.start()
        return cp

    mine = pl.ds(pl.multiple_of(a * half, half), half)
    other = pl.ds(pl.multiple_of((1 - a) * half, half), half)

    sib_of = remote(of.at[a], of.at[a], sib)
    sib_g = remote(own.at[:, :, other], g.at[0, a], sib)
    keep = local(own.at[:, :, mine], g.at[0, a], 0)
    keep.wait()
    sib_g.wait_recv()

    wrap = x < 2
    d1, d2 = dev(xx=step(x, -1)), dev(xx=step(x, -2))
    wrap1 = x < 1
    nowrap1, nowrap2 = x >= 1, x >= 2
    up = dev(zz=step(zl, -1))

    def shift_z(u):
        return remote(g.at[u, 0:2], g.at[u, 6:8], up, when=wrap)

    def shift_x(u, field_at, first, second):
        r1, r2 = first
        w1, w2 = second
        return (remote(g.at[u, field_at:field_at + 2], g.at[u, 2:4], d1, when=w1, rsem_at=r1),
                remote(g.at[u, field_at:field_at + 2], g.at[u, 4:6], d2, when=w2, rsem_at=r2))

    def spread_s(u):
        cps = []
        for d in (1, 2, 3):
            yd = step(y, d)
            dst = sl.at[a, y] if u == 0 else sb.at[y]
            cps.append(remote(g.at[u, yd // 2], dst, dev(yy=yd)))
        return cps

    def spread_t(u):
        cps = []
        for d in (1, 2, 3):
            yd = step(y, d)
            dst = tl.at[a, y] if u == 0 else tb.at[y]
            cps.append(remote(tsel.at[u, yd], dst, dev(yy=yd)))
        return cps

    xsem = [(psem.at[4 + 2 * u], psem.at[5 + 2 * u]) for u in range(2)]
    z0 = shift_z(0)
    x0 = shift_x(0, 0, xsem[0], (nowrap1, nowrap2))
    s0 = spread_s(0)
    own_s0 = local(g.at[0, y // 2], sl.at[a, y], 1)
    cross = remote(g.at[0, 0:2], g.at[1, 0:2], dev(hh=1 - h))
    pl.when(wrap)(z0.wait_recv)
    w0 = shift_x(0, 6, xsem[0], (wrap1, wrap))
    sib_of.wait_recv()

    def forward(dst, index):
        return remote(dst.at[a, index], dst.at[a, index], sib)

    own_s0.wait()
    fs = [forward(sl, y)]
    for d in (1, 2, 3):
        s0[d - 1].wait_recv()
        fs.append(forward(sl, step(y, -d)))

    def select(u):
        def body(i, carry):
            ri = i // (rows // 8)
            at = pl.ds(pl.multiple_of((i % (rows // 8)) * 8, 8), 8)
            cand = [g[u, f, ri, at, :] for f in range(1, 6)]
            for p in range(4):
                first = p // 2
                m = of[first, p % 2]
                v = cand[first + 3]
                for o in (3, 2, 1):
                    v = jnp.where(m == F32(o), cand[first + o - 1], v)
                tsel[u, p, ri, at, :] = v
            return carry
        lax.fori_loop(0, 2 * rows // 8, body, 0)

    x0[0].wait_recv()
    x0[1].wait_recv()
    select(0)
    t0 = spread_t(0)
    own_t0 = local(tsel.at[0, y], tl.at[a, y], 2)

    cross.wait_recv()
    z1 = shift_z(1)
    x1 = shift_x(1, 0, xsem[1], (nowrap1, nowrap2))
    s1 = spread_s(1)
    own_s1 = local(g.at[1, y // 2], sb.at[y], 3)
    pl.when(wrap)(z1.wait_recv)
    w1 = shift_x(1, 6, xsem[1], (wrap1, wrap))

    own_t0.wait()
    ft = [forward(tl, y)]
    for d in (1, 2, 3):
        t0[d - 1].wait_recv()
        ft.append(forward(tl, step(y, -d)))

    def prepare_left(src, dst, ch, yi):
        at = pl.ds(pl.multiple_of(yi * rows, rows), rows)
        for ri in range(2):
            for yb in range(4):
                hi, lo = split(src[ch, yi, ri, :, yb * rows:(yb + 1) * rows])
                cols = slice((2 * yb + ri) * rows, (2 * yb + ri + 1) * rows)
                dst[0, ch, at, cols] = hi
                dst[1, ch, at, cols] = lo

    def prepare_right(block, dst, yi):
        at0 = pl.ds(pl.multiple_of(yi * 2 * rows, rows), rows)
        at1 = pl.ds(pl.multiple_of(yi * 2 * rows + rows, rows), rows)
        rh, rl = split(block[0])
        ih, il = split(block[1])
        for part_at, re, im in ((0, rh, ih), (1, rl, il)):
            dst[part_at, 0, at0, :] = re
            dst[part_at, 0, at1, :] = -im
            dst[part_at, 1, at0, :] = im
            dst[part_at, 1, at1, :] = re

    tile_m, tile_n = 2 * rows, 2 * rows

    def multiply(left, ch, right, acc, fresh):
        def body(i, carry):
            ri = i // 4
            mt = pl.ds(pl.multiple_of(((i // 2) % 2) * tile_m, tile_m), tile_m)
            nt = pl.ds(pl.multiple_of((i % 2) * tile_n, tile_n), tile_n)
            lh = left[0, ch, mt, :]
            ll = left[1, ch, mt, :]
            rh = right[0, ri, :, nt]
            rl = right[1, ri, :, nt]
            r = jnp.dot(lh, rh, preferred_element_type=F32)
            r += jnp.dot(lh, rl, preferred_element_type=F32)
            r += jnp.dot(ll, rh, preferred_element_type=F32)
            if fresh:
                acc[ri, mt, nt] = r
            else:
                acc[ri, mt, nt] += r
            return carry
        lax.fori_loop(0, 8, body, 0)

    def each_block(fn):
        def body(i, carry):
            fn(i)
            return carry
        lax.fori_loop(0, 4, body, 0)

    for cp in fs:
        cp.wait_recv()

    def prep_s(i):
        prepare_left(sl, ls, 0, i)
        prepare_left(sl, ls, 1, i)
        prepare_right(sl.at[a, i], rs, i)
    each_block(prep_s)

    for cp in ft:
        cp.wait_recv()

    def prep_t(i):
        prepare_left(tl, lt, 0, i)
        prepare_left(tl, lt, 1, i)
        prepare_right(tl.at[a, i], rt, i)
    each_block(prep_t)

    multiply(ls, h, rt, pacc, True)
    multiply(lt, h, rs, qacc, True)

    x1[0].wait_recv()
    x1[1].wait_recv()
    select(1)
    t1 = spread_t(1)
    own_t1 = local(tsel.at[1, y], tb.at[y], 4)

    own_s1.wait()
    for cp in s1:
        cp.wait_recv()
    each_block(lambda i: prepare_right(sb.at[i], rs, i))
    multiply(lt, 1 - h, rs, qacc, False)

    own_t1.wait()
    for cp in t1:
        cp.wait_recv()
    each_block(lambda i: prepare_right(tb.at[i], rt, i))
    multiply(ls, 1 - h, rt, pacc, False)

    src_core = y // 2
    k = y % 2
    home = src_core == a
    away = src_core != a
    for d in range(4):
        yd = step(y, d)
        src = pacc.at[:, pl.ds(pl.multiple_of(yd * rows, rows), rows), :]
        dst = out.at[k, :, :, mine]
        if d == 0:
            lcp = pltpu.make_async_copy(src, dst, lsem.at[5])
            pl.when(home)(lcp.start)
            remote(src, dst, sib, when=away, rsem_at=psem.at[2 * k + a])
        else:
            remote(src, dst, dev(core=src_core, yy=yd), rsem_at=psem.at[2 * k + a])

    def tr_body(i, acc):
        ri = i // (4 * rows // 8)
        at = pl.ds(pl.multiple_of((i % (4 * rows // 8)) * 8, 8), 8)
        return acc + pacc[ri, at, :] * qacc[ri, at, :]
    acc = lax.fori_loop(0, 2 * 4 * rows // 8, tr_body, jnp.zeros((8, half), F32))
    lanes = part.shape[1]
    tot = acc[:, 0:lanes]
    for j in range(1, half // lanes):
        tot += acc[:, j * lanes:(j + 1) * lanes]
    part[...] = tot
    slot = 2 * h + a
    for dh in range(2):
        for d in range(4):
            dst = parts.at[k, slot]
            if d == 0 and dh == 0:
                @pl.when(home)
                def _():
                    parts[k, slot] = part[...]
                remote(part, dst, sib, when=away, rsem_at=trsem.at[k, slot])
            else:
                remote(part, dst, dev(core=src_core, yy=step(y, d), hh=(h + dh) % 2), rsem_at=trsem.at[k, slot])

    for kk in range(2):
        for ch in range(2):
            for hh in range(2):
                i = 2 * hh + ch
                own_slot = (y == 2 * a + kk) & (ch == a) & (hh == h)
                cp = pltpu.make_async_remote_copy(src_ref=part, dst_ref=parts.at[kk, i], send_sem=ssem.at[0], recv_sem=trsem.at[kk, i], device_id=sib, device_id_type=MESH)
                pl.when(jnp.logical_not(own_slot))(cp.wait_recv)
    width = F32(8 * rows)
    for kk in range(2):
        total = parts[kk, 0] + parts[kk, 1] + parts[kk, 2] + parts[kk, 3]
        corr[kk] = jnp.broadcast_to(jnp.sum(total) / width, corr.shape[1:])

    for kk in range(2):
        for ch in range(2):
            own_slot = (y == 2 * a + kk) & (ch == a)
            cp = pltpu.make_async_remote_copy(
                src_ref=pacc.at[:, 0:rows, :], dst_ref=out.at[kk, :, :, ch * half:(ch + 1) * half],
                send_sem=ssem.at[0], recv_sem=psem.at[2 * kk + ch], device_id=sib, device_id_type=MESH)
            pl.when(jnp.logical_not(own_slot))(cp.wait_recv)
    pl.when(home)(lcp.wait)
    for cp, when in sends:
        if when is None:
            cp.wait_send()
        else:
            pl.when(when)(cp.wait_send)


NSEM = 64


def body(fields, offsets):
    own = fields[0]
    rows, width = own.shape[1], own.shape[2]
    half = width // 2
    block = (2, rows, half)
    out, corr = pl.pallas_call(
        functools.partial(kernel, rows),
        out_shape=(jax.ShapeDtypeStruct((2, 2, rows, width), F32), jax.ShapeDtypeStruct((2, 8, 128), F32)),
        in_specs=[pl.BlockSpec(memory_space=pl.ANY), pl.BlockSpec(memory_space=pltpu.SMEM)],
        out_specs=(pl.BlockSpec(memory_space=pl.ANY), pl.BlockSpec(memory_space=pltpu.VMEM)),
        scratch_shapes=[
            pltpu.VMEM((2, 8) + block, F32),
            pltpu.VMEM((2, 2, 8, half), F32),
            pltpu.VMEM((2, 4) + block, F32),
            pltpu.VMEM((2, 4) + block, F32),
            pltpu.VMEM((2, 4) + block, F32),
            pltpu.VMEM((4,) + block, F32),
            pltpu.VMEM((4,) + block, F32),
            pltpu.VMEM((2, 2, half, width), BF16),
            pltpu.VMEM((2, 2, half, width), BF16),
            pltpu.VMEM((2, 2, width, half), BF16),
            pltpu.VMEM((2, 2, width, half), BF16),
            pltpu.VMEM((2, half, half), F32),
            pltpu.VMEM((2, half, half), F32),
            pltpu.VMEM((8, 128), F32),
            pltpu.VMEM((2, 4, 8, 128), F32),
            pltpu.SemaphoreType.DMA((NSEM,)),
            pltpu.SemaphoreType.DMA((NSEM,)),
            pltpu.SemaphoreType.DMA((8,)),
            pltpu.SemaphoreType.DMA((2, 4)),
            pltpu.SemaphoreType.DMA((8,)),
        ],
        compiler_params=pltpu.CompilerParams(collective_id=0, has_side_effects=True, vmem_limit_bytes=60 * 2**20),
        cost_estimate=pl.CostEstimate(flops=13 * 10**9, bytes_accessed=4 * 2**20, transcendentals=0),
        name="contract",
    )(own, offsets)
    return out[None], corr[:, 0, 0][None]


def solution(mesh):
    in_specs = (P("tm", None, "mode", None), P("tm", None))
    out_specs = (P("tm", None, None, "mode", None), P("tm", None))
    return jax.shard_map(body, mesh=mesh, in_specs=in_specs, out_specs=out_specs, check_vma=False)
```

time: 636 us -> 216 us (0.34); the launches traced: 626 us -> 216 us
  waiting for transfers between devices: 500 us -> 0 us
  Pallas kernels: 0 us -> 211 us
  matrix products: 67.1 us -> 0 us
  blocking collectives: 23 us -> 0 us
  between operations: 19.8 us -> 0.64 us
  starting transfers between devices: 9.18 us -> 0 us
    all_gather x2 -> x0, waiting for transfers between devices: 446 us -> none  [the longest x1 328 us: body(): piece = lax.all_gather(sinks, 'mode', axis=2, tiled=True)]
    pallas_call x0 -> x1, Pallas kernels: none -> 211 us  [body(): pl.pallas_call(functools.partial(kernel, rows), out_shape=(jax.ShapeDtype...]
    dot_general x8 -> x0, matrix products: 67.1 us -> none  [the longest x1 10.1 us: body(): jnp.einsum('krc,cn->krn', left_re, piece[1], precision=hi)]
    ppermute x4 -> x0, waiting for transfers between devices: 53.6 us -> none  [passed_along(): return lax.ppermute(block, axis, route)]
    psum x1 -> x0, blocking collectives: 23 us -> none  [body(): traces = lax.psum(partial_trace, 'mode')]
    ppermute x4 -> x0, starting transfers between devices: 9.1 us -> none  [passed_along(): return lax.ppermute(block, axis, route)]
  transfers between devices with their start and end apart: 6 -> 0, of which waited for: 5 -> 0; matrix products, arithmetic and copies ran while one was open for 6% -> 0% of each run, Pallas kernels for 0% -> 0%
where the time goes in v1:
time: 216 us
  Pallas kernels  211 us (98%)
  local copies, waits for them, and re-layouts  4.46 us (2%)
    pallas_call x1, Pallas kernels, body(): pl.pallas_call(functools.partial(kernel, rows), out_shape=(jax.ShapeDtype...  211 us

profile of v1, /device:TPU:7, one launch (start us, length us, event | category | flops | bytes accessed | tf_op | source)
XLA Modules:
  0.0 215.7 jit_solution(15810296846795853852)
XLA Ops:
  0.6 210.6 %contract.1 = (f32[2,2,128,1024]{3,2,1,0:T(8,128)}, f32[2,8,128]{2,1,0:T(8,128)}) custom-call(f32[2,128,1024]{2,1,0:T(8,128)} %bitcast.4, s32[1,2]{1,0:T(1,128)} %offs.1), custom_call_target="tpu_custom_call" | custom-call | flops 12999999488 | bytes 4194304 | tf_op jit(solution)/shard_map/contract/pallas_call | solution.py:332
  211.2 1.3 slice_reduce_fusion
  212.5 3.2 %copy.5 = f32[1,2,2,128,1024]{4,3,2,1,0:T(8,128)} copy(f32[1,2,2,128,1024]{4,3,2,1,0:T(8,128)} %bitcast.3) | data formatting | bytes 4194304

commit v2 on v0

v2 whole, which is shorter than its diff:
```python
import functools

import jax
import jax.numpy as jnp
from jax import lax
from jax.experimental import pallas as pl
from jax.experimental.pallas import tpu as pltpu
from jax.sharding import PartitionSpec as P

MESH = pl.DeviceIdType.MESH
F32 = jnp.float32
BF16 = jnp.bfloat16
NX, NY, NC = 4, 4, 4
NSEM = 192


def split(value):
    hi = value.astype(BF16)
    lo = (value - hi.astype(F32)).astype(BF16)
    return hi, lo


def kernel(rows, own, offs, out, corr, g, of, tsel, sl, tl, sb, tb, ls, lt, rs, rt, pacc, qacc, part, parts,
           ssem, rsem, xsem, psem, trsem, lsem):
    wide = 128
    half = NC * wide
    tm = lax.axis_index("tm")
    mode = lax.axis_index("mode")
    a = tm % 2
    x = (tm // 2) % NX
    zl = tm // (2 * NX)
    y = mode % NY
    h = mode // NY

    def dev(core=a, xx=x, zz=zl, yy=y, hh=h):
        return ((zz * NX + xx) * 2 + core, hh * NY + yy)

    def step(v, d):
        return (v + d + 4) % 4

    sib = dev(core=1 - a)

    bar = pltpu.get_barrier_semaphore()
    count = 0

    def greet(device):
        pl.semaphore_signal(bar, 1, device_id=device, device_id_type=MESH)

    for dh in (1, 0):
        for dc in range(2):
            for dy in range(4):
                if dc or dh or dy:
                    greet(dev(core=(a + dc) % 2, yy=step(y, dy), hh=(h + dh) % 2))
                    count += 1
    for d in (1, 3):
        greet(dev(zz=step(zl, d)))
        count += 1
    for d in (1, 2, 3):
        greet(dev(xx=step(x, d)))
        count += 1

    def columns(core, c):
        return pl.ds(pl.multiple_of(core * half + c * wide, wide), wide)

    nlocal = [0]

    def local(src, dst):
        cp = pltpu.make_async_copy(src, dst, lsem.at[nlocal[0]])
        nlocal[0] += 1
        cp.start()
        return cp

    keep = [local(own.at[:, :, columns(a, c)], g.at[0, c, a]) for c in range(NC)]
    for k in range(2):
        of[a, k] = jnp.full(of.shape[2:], offs[0, k].astype(F32), F32)
    pl.semaphore_wait(bar, count)

    sends = []
    counter = [0]

    def remote(src, dst, device, when=None, at=None):
        i = counter[0]
        counter[0] += 1
        cp = pltpu.make_async_remote_copy(
            src_ref=src, dst_ref=dst, send_sem=ssem.at[i], recv_sem=rsem.at[i] if at is None else at,
            device_id=device, device_id_type=MESH)
        if when is None:
            cp.start()
        else:
            pl.when(when)(cp.start)
        sends.append((cp, when))
        return cp

    sib_of = remote(of.at[a], of.at[a], sib)
    sib_g = [remote(own.at[:, :, columns(1 - a, c)], g.at[0, c, a], sib) for c in range(NC)]

    wrap1, wrap2 = x < 1, x < 2
    plain1, plain2 = x >= 1, x >= 2
    d1, d2, up, across = dev(xx=step(x, -1)), dev(xx=step(x, -2)), dev(zz=step(zl, -1)), dev(hh=1 - h)

    def shift_z(u, c):
        return remote(g.at[u, c, 0:2], g.at[u, c, 6:8], up, when=wrap2)

    def shift_x(u, c, field, when1, when2):
        cp1 = remote(g.at[u, c, field:field + 2], g.at[u, c, 2:4], d1, when=when1, at=xsem.at[u, c, 0])
        cp2 = remote(g.at[u, c, field:field + 2], g.at[u, c, 4:6], d2, when=when2, at=xsem.at[u, c, 1])
        return cp1, cp2

    def spread(src, dst):
        return [remote(src(step(y, d)), dst, dev(yy=step(y, d))) for d in (1, 2, 3)]

    def wait_all(cps):
        for cp in cps:
            cp.wait_recv()

    def select(u, c):
        def body(i, carry):
            at = pl.ds(pl.multiple_of(i * 8, 8), 8)
            for ri in range(2):
                cand = [g[u, c, f, ri, at, :] for f in range(1, 6)]
                for p in range(4):
                    first = p // 2
                    m = of[first, p % 2]
                    v = cand[first + 3]
                    for o in (3, 2, 1):
                        v = jnp.where(m == F32(o), cand[first + o - 1], v)
                    tsel[u, c, p, ri, at, :] = v
            return carry
        lax.fori_loop(0, rows // 8, body, 0)

    z, xc, s0, t0, cross, s1, t1 = {}, {}, [], {}, {}, {}, {}
    for c in range(NC):
        keep[c].wait()
        sib_g[c].wait_recv()
        z[0, c] = shift_z(0, c)
        xc[0, c] = shift_x(0, c, 0, plain1, plain2)
        cross[c] = remote(g.at[0, c, 0:2], g.at[1, c, 0:2], across)
    s0 = spread(lambda yd: g.at[0, :, yd // 2], sl.at[a, y])
    own_s0 = local(g.at[0, :, y // 2], sl.at[a, y])
    sib_of.wait_recv()
    own_t0, own_s1, own_t1 = [], [], []
    fs, ft = [], []
    for c in range(NC):
        pl.when(wrap2)(z[0, c].wait_recv)
        shift_x(0, c, 6, wrap1, wrap2)
        wait_all(xc[0, c])
        select(0, c)
        t0[c] = spread(lambda yd: tsel.at[0, c, yd], tl.at[a, y, c])
        own_t0.append(local(tsel.at[0, c, y], tl.at[a, y, c]))
        cross[c].wait_recv()
        z[1, c] = shift_z(1, c)
        xc[1, c] = shift_x(1, c, 0, plain1, plain2)
        s1[c] = spread(lambda yd: g.at[1, c, yd // 2], sb.at[y, c])
        own_s1.append(local(g.at[1, c, y // 2], sb.at[y, c]))

    def forward(dst, index):
        return remote(dst.at[a, index], dst.at[a, index], sib)

    own_s0.wait()
    fs.append(forward(sl, y))
    for d in (1, 2, 3):
        s0[d - 1].wait_recv()
        fs.append(forward(sl, step(y, -d)))

    def prepare_left(src, dst, ch, yi):
        at = pl.ds(pl.multiple_of(yi * rows, rows), rows)
        for ri in range(2):
            for c in range(NC):
                hi, lo = split(src[ch, yi, c, ri])
                cols = slice((2 * c + ri) * wide, (2 * c + ri + 1) * wide)
                dst[0, ch, at, cols] = hi
                dst[1, ch, at, cols] = lo

    def prepare_right(src, dst, yi, c):
        at0 = pl.ds(pl.multiple_of(yi * 2 * rows, rows), rows)
        at1 = pl.ds(pl.multiple_of(yi * 2 * rows + rows, rows), rows)
        rh, rl = split(src[yi, c, 0])
        ih, il = split(src[yi, c, 1])
        for n, re, im in ((0, rh, ih), (1, rl, il)):
            dst[n, c, at0, 0:wide] = re
            dst[n, c, at0, wide:2 * wide] = im
            dst[n, c, at1, 0:wide] = -im
            dst[n, c, at1, wide:2 * wide] = re

    tile = 2 * rows

    def multiply(left, ch, right, acc, fresh, first, last):
        def body(i, carry):
            c = i // 2
            mt = pl.ds(pl.multiple_of((i % 2) * tile, tile), tile)
            lh = left[0, ch, mt, :]
            rh = right[0, c]
            r = jnp.dot(lh, rh, preferred_element_type=F32)
            r += jnp.dot(lh, right[1, c], preferred_element_type=F32)
            r += jnp.dot(left[1, ch, mt, :], rh, preferred_element_type=F32)
            for ri in range(2):
                v = r[:, ri * wide:(ri + 1) * wide]
                acc[c, ri, mt, :] = v if fresh else acc[c, ri, mt, :] + v
            return carry
        lax.fori_loop(2 * first, 2 * last, body, 0)

    def loop(n, fn):
        def body(i, carry):
            fn(i)
            return carry
        lax.fori_loop(0, n, body, 0)

    def prep_s(i):
        prepare_left(sl, ls, 0, i)
        prepare_left(sl, ls, 1, i)

    def prep_t(i):
        prepare_left(tl, lt, 0, i)
        prepare_left(tl, lt, 1, i)

    for c in range(NC):
        pl.when(wrap2)(z[1, c].wait_recv)
        shift_x(1, c, 6, wrap1, wrap2)
        wait_all(xc[1, c])
        select(1, c)
        t1[c] = spread(lambda yd: tsel.at[1, c, yd], tb.at[y, c])
        own_t1.append(local(tsel.at[1, c, y], tb.at[y, c]))
        if c == 0:
            for cp in own_t0:
                cp.wait()
            ft.append(forward(tl, y))
            for d in (1, 2, 3):
                for cc in range(NC):
                    t0[cc][d - 1].wait_recv()
                ft.append(forward(tl, step(y, -d)))
            wait_all(fs)
            loop(4, prep_s)
            loop(16, lambda i: prepare_right(sl.at[a], rs, i // NC, i % NC))
        if c == 1:
            wait_all(ft)
            loop(4, prep_t)
            loop(16, lambda i: prepare_right(tl.at[a], rt, i // NC, i % NC))
            multiply(ls, h, rt, pacc, True, 0, NC)
        if c == 2:
            multiply(lt, h, rs, qacc, True, 0, NC)

    for c in range(NC):
        own_s1[c].wait()
        wait_all(s1[c])
    loop(16, lambda i: prepare_right(sb, rs, i // NC, i % NC))
    multiply(lt, 1 - h, rs, qacc, False, 0, NC)

    src_core = y // 2
    k = y % 2
    home = src_core == a
    away = src_core != a
    total = jnp.zeros((8, wide), F32)
    back = []
    for c in range(NC):
        own_t1[c].wait()
        wait_all(t1[c])
        loop(4, lambda i: prepare_right(tb, rt, i, c))
        multiply(ls, 1 - h, rt, pacc, False, c, c + 1)
        for d in (1, 2, 3, 0):
            yd = step(y, d)
            src = pacc.at[c, :, pl.ds(pl.multiple_of(yd * rows, rows), rows), :]
            dst = out.at[k, :, :, columns(a, c)]
            if d == 0:
                lcp = pltpu.make_async_copy(src, dst, lsem.at[20 + c])
                pl.when(home)(lcp.start)
                back.append(lcp)
                remote(src, dst, sib, when=away, at=psem.at[k, a, c])
            else:
                remote(src, dst, dev(core=src_core, yy=yd), at=psem.at[k, a, c])

        def tr_body(i, acc):
            at = pl.ds(pl.multiple_of(i * 8, 8), 8)
            for ri in range(2):
                acc = acc + pacc[c, ri, at, :] * qacc[c, ri, at, :]
            return acc
        total = lax.fori_loop(0, 4 * rows // 8, tr_body, total)

    part[...] = total
    slot = 2 * h + a
    for dh in (1, 0):
        for d in (1, 2, 3, 0):
            dst = parts.at[k, slot]
            if d == 0 and dh == 0:
                @pl.when(home)
                def _():
                    parts[k, slot] = part[...]
                remote(part, dst, sib, when=away, at=trsem.at[k, slot])
            else:
                remote(part, dst, dev(core=src_core, yy=step(y, d), hh=(h + dh) % 2), at=trsem.at[k, slot])

    def expect(dst, sem, unless):
        cp = pltpu.make_async_remote_copy(src_ref=dst, dst_ref=dst, send_sem=ssem.at[0], recv_sem=sem, device_id=sib, device_id_type=MESH)
        pl.when(jnp.logical_not(unless))(cp.wait_recv)

    for kk in range(2):
        for ch in range(2):
            for hh in range(2):
                expect(parts.at[kk, 2 * hh + ch], trsem.at[kk, 2 * hh + ch], (y == 2 * a + kk) & (ch == a) & (hh == h))
    width = F32(8 * rows)
    for kk in range(2):
        trace = parts[kk, 0] + parts[kk, 1] + parts[kk, 2] + parts[kk, 3]
        corr[kk] = jnp.broadcast_to(jnp.sum(trace) / width, corr.shape[1:])

    for kk in range(2):
        for ch in range(2):
            for c in range(NC):
                expect(out.at[kk, :, :, columns(ch, c)], psem.at[kk, ch, c], (y == 2 * a + kk) & (ch == a))
    for lcp in back:
        pl.when(home)(lcp.wait)
    for cp, when in sends:
        if when is None:
            cp.wait_send()
        else:
            pl.when(when)(cp.wait_send)


def body(fields, offsets):
    own = fields[0]
    rows, width = own.shape[1], own.shape[2]
    half = width // 2
    block = (2, rows, 128)
    out, corr = pl.pallas_call(
        functools.partial(kernel, rows),
        out_shape=(jax.ShapeDtypeStruct((2, 2, rows, width), F32), jax.ShapeDtypeStruct((2, 8, 128), F32)),
        in_specs=[pl.BlockSpec(memory_space=pl.ANY), pl.BlockSpec(memory_space=pltpu.SMEM)],
        out_specs=(pl.BlockSpec(memory_space=pl.ANY), pl.BlockSpec(memory_space=pltpu.VMEM)),
        scratch_shapes=[
            pltpu.VMEM((2, NC, 8) + block, F32),
            pltpu.VMEM((2, 2, 8, 128), F32),
            pltpu.VMEM((2, NC, 4) + block, F32),
            pltpu.VMEM((2, 4, NC) + block, F32),
            pltpu.VMEM((2, 4, NC) + block, F32),
            pltpu.VMEM((4, NC) + block, F32),
            pltpu.VMEM((4, NC) + block, F32),
            pltpu.VMEM((2, 2, half, width), BF16),
            pltpu.VMEM((2, 2, half, width), BF16),
            pltpu.VMEM((2, NC, width, 256), BF16),
            pltpu.VMEM((2, NC, width, 256), BF16),
            pltpu.VMEM((NC, 2, half, 128), F32),
            pltpu.VMEM((NC, 2, half, 128), F32),
            pltpu.VMEM((8, 128), F32),
            pltpu.VMEM((2, 4, 8, 128), F32),
            pltpu.SemaphoreType.DMA((NSEM,)),
            pltpu.SemaphoreType.DMA((NSEM,)),
            pltpu.SemaphoreType.DMA((2, NC, 2)),
            pltpu.SemaphoreType.DMA((2, 2, NC)),
            pltpu.SemaphoreType.DMA((2, 4)),
            pltpu.SemaphoreType.DMA((24,)),
        ],
        compiler_params=pltpu.CompilerParams(collective_id=0, has_side_effects=True, vmem_limit_bytes=60 * 2**20),
        cost_estimate=pl.CostEstimate(flops=13 * 10**9, bytes_accessed=4 * 2**20, transcendentals=0),
        name="contract",
    )(own, offsets)
    return out[None], corr[:, 0, 0][None]


def solution(mesh):
    in_specs = (P("tm", None, "mode", None), P("tm", None))
    out_specs = (P("tm", None, None, "mode", None), P("tm", None))
    return jax.shard_map(body, mesh=mesh, in_specs=in_specs, out_specs=out_specs, check_vma=False)
```

time: 636 us -> 176 us (0.28); the launches traced: 626 us -> 176 us
  waiting for transfers between devices: 500 us -> 0 us
  Pallas kernels: 0 us -> 171 us
  matrix products: 67.1 us -> 0 us
  blocking collectives: 23 us -> 0 us
  between operations: 19.8 us -> 0.64 us
  starting transfers between devices: 9.18 us -> 0 us
    all_gather x2 -> x0, waiting for transfers between devices: 446 us -> none  [the longest x1 328 us: body(): piece = lax.all_gather(sinks, 'mode', axis=2, tiled=True)]
    pallas_call x0 -> x1, Pallas kernels: none -> 171 us  [body(): pl.pallas_call(functools.partial(kernel, rows), out_shape=(jax.ShapeDtype...]
    dot_general x8 -> x0, matrix products: 67.1 us -> none  [the longest x1 10.1 us: body(): jnp.einsum('krc,cn->krn', left_re, piece[1], precision=hi)]
    ppermute x4 -> x0, waiting for transfers between devices: 53.6 us -> none  [passed_along(): return lax.ppermute(block, axis, route)]
    psum x1 -> x0, blocking collectives: 23 us -> none  [body(): traces = lax.psum(partial_trace, 'mode')]
    ppermute x4 -> x0, starting transfers between devices: 9.1 us -> none  [passed_along(): return lax.ppermute(block, axis, route)]
  transfers between devices with their start and end apart: 6 -> 0, of which waited for: 5 -> 0; matrix products, arithmetic and copies ran while one was open for 6% -> 0% of each run, Pallas kernels for 0% -> 0%
where the time goes in v2:
time: 176 us
  Pallas kernels  171 us (97%)
  local copies, waits for them, and re-layouts  4.46 us (3%)
    pallas_call x1, Pallas kernels, body(): pl.pallas_call(functools.partial(kernel, rows), out_shape=(jax.ShapeDtype...  171 us

profile of v2, /device:TPU:7, one launch (start us, length us, event | category | flops | bytes accessed | tf_op | source)
XLA Modules:
  0.0 176.1 jit_solution(12745306370946009286)
XLA Ops:
  0.6 171.0 %contract.1 = (f32[2,2,128,1024]{3,2,1,0:T(8,128)}, f32[2,8,128]{2,1,0:T(8,128)}) custom-call(f32[2,128,1024]{2,1,0:T(8,128)} %bitcast.4, s32[1,2]{1,0:T(1,128)} %offs.1), custom_call_target="tpu_custom_call" | custom-call | flops 12999999488 | bytes 4194304 | tf_op jit(solution)/shard_map/contract/pallas_call | solution.py:322
  171.6 1.3 slice_reduce_fusion
  172.9 3.2 %copy.5 = f32[1,2,2,128,1024]{4,3,2,1,0:T(8,128)} copy(f32[1,2,2,128,1024]{4,3,2,1,0:T(8,128)} %bitcast.3) | data formatting | bytes 4194304

commit v3 on v2

--- a/solution.py
+++ b/solution.py
@@ -11,7 +11,8 @@
 F32 = jnp.float32
 BF16 = jnp.bfloat16
 NX, NY, NC = 4, 4, 4
-NSEM = 192
+NSEM = 224
+VIA_HIGH, VIA_LOW = (0, 1), (2, 3)
 
 
 def split(value):
@@ -21,7 +22,7 @@
 
 
 def kernel(rows, own, offs, out, corr, g, of, tsel, sl, tl, sb, tb, ls, lt, rs, rt, pacc, qacc, part, parts,
-           ssem, rsem, xsem, psem, trsem, lsem):
+           ssem, rsem, bsem, xsem, psem, trsem, lsem):
     wide = 128
     half = NC * wide
     tm = lax.axis_index("tm")
@@ -52,9 +53,10 @@
                 if dc or dh or dy:
                     greet(dev(core=(a + dc) % 2, yy=step(y, dy), hh=(h + dh) % 2))
                     count += 1
-    for d in (1, 3):
-        greet(dev(zz=step(zl, d)))
-        count += 1
+    for dz in (1, -1):
+        greet(dev(zz=step(zl, dz)))
+        greet(dev(xx=step(x, -dz), zz=step(zl, dz)))
+        count += 2
     for d in (1, 2, 3):
         greet(dev(xx=step(x, d)))
         count += 1
@@ -64,10 +66,18 @@
 
     nlocal = [0]
 
-    def local(src, dst):
-        cp = pltpu.make_async_copy(src, dst, lsem.at[nlocal[0]])
-        nlocal[0] += 1
-        cp.start()
+    def begin(cp, when):
+        if when is None:
+            cp.start()
+        else:
+            pl.when(when)(cp.start)
+
+    def local(src, dst, when=None, at=None):
+        if at is None:
+            at = nlocal[0]
+            nlocal[0] += 1
+        cp = pltpu.make_async_copy(src, dst, lsem.at[at])
+        begin(cp, when)
         return cp
 
     keep = [local(own.at[:, :, columns(a, c)], g.at[0, c, a]) for c in range(NC)]
@@ -84,30 +94,56 @@
         cp = pltpu.make_async_remote_copy(
             src_ref=src, dst_ref=dst, send_sem=ssem.at[i], recv_sem=rsem.at[i] if at is None else at,
             device_id=device, device_id_type=MESH)
-        if when is None:
-            cp.start()
-        else:
-            pl.when(when)(cp.start)
+        begin(cp, when)
         sends.append((cp, when))
         return cp
 
     sib_of = remote(of.at[a], of.at[a], sib)
     sib_g = [remote(own.at[:, :, columns(1 - a, c)], g.at[0, c, a], sib) for c in range(NC)]
 
-    wrap1, wrap2 = x < 1, x < 2
-    plain1, plain2 = x >= 1, x >= 2
+    low, high, second, last = x < 2, x >= 2, x == 2, x == 3
     d1, d2, up, across = dev(xx=step(x, -1)), dev(xx=step(x, -2)), dev(zz=step(zl, -1)), dev(hh=1 - h)
-
-    def shift_z(u, c):
-        return remote(g.at[u, c, 0:2], g.at[u, c, 6:8], up, when=wrap2)
-
-    def shift_x(u, c, field, when1, when2):
-        cp1 = remote(g.at[u, c, field:field + 2], g.at[u, c, 2:4], d1, when=when1, at=xsem.at[u, c, 0])
-        cp2 = remote(g.at[u, c, field:field + 2], g.at[u, c, 4:6], d2, when=when2, at=xsem.at[u, c, 1])
-        return cp1, cp2
-
-    def spread(src, dst):
-        return [remote(src(step(y, d)), dst, dev(yy=step(y, d))) for d in (1, 2, 3)]
+    firsts, seconds, behind, lent = {}, {}, {}, {}
+
+    def to_first(u, c, field, when):
+        firsts[u, c] = remote(g.at[u, c, field:field + 2], g.at[u, c, 2:4], d1, when=when, at=xsem.at[u, c, 0])
+
+    def to_second(u, c, field, when):
+        seconds[u, c] = remote(g.at[u, c, field:field + 2], g.at[u, c, 4:6], d2, when=when, at=xsem.at[u, c, 1])
+
+    def relay_first(u, c, when):
+        remote(g.at[u, c, 2:4], g.at[u, c, 4:6], dev(xx=step(x, -1)), when=when, at=xsem.at[u, c, 1])
+
+    def shift_z(u, c, when):
+        behind[u, c] = remote(g.at[u, c, 0:2], g.at[u, c, 6:8], up, when=when)
+
+    def lend(u, c, when):
+        lent[u, c] = remote(g.at[u, c, 0:2], g.at[u, c, 6:8], dev(xx=3 - x), when=when)
+
+    def pass_back(u, c):
+        pl.when(high)(lent[u, c].wait_recv)
+        at = jnp.where(last, 0, 1)
+        remote(g.at[u, c, 6:8], g.at[u, c, pl.ds(2 + 2 * at, 2)], dev(xx=3, zz=step(zl, -1)), when=high, at=xsem.at[u, c, at])
+
+    def hand_on(u, c, when):
+        pl.when(when)(firsts[u, c].wait_recv)
+        relay_first(u, c, when)
+
+    def bring_on(u, c):
+        pl.when(low)(behind[u, c].wait_recv)
+        to_first(u, c, 6, x == 0)
+        to_second(u, c, 6, low)
+
+    def arrived_first(u, c):
+        if c in VIA_LOW:
+            if u == 0:
+                bring_on(u, c)
+            firsts[u, c].wait_recv()
+        else:
+            pl.when(low)(firsts[u, c].wait_recv)
+
+    def spread(src, dst, when=None, at=None):
+        return [remote(src(step(y, d)), dst, dev(yy=step(y, d)), when=when, at=None if at is None else at(d)) for d in (1, 2, 3)]
 
     def wait_all(cps):
         for cp in cps:
@@ -128,30 +164,59 @@
             return carry
         lax.fori_loop(0, rows // 8, body, 0)
 
-    z, xc, s0, t0, cross, s1, t1 = {}, {}, [], {}, {}, {}, {}
+    t0, cross, s1, t1 = {}, {}, {}, {}
+    own_t0, own_s1, own_t1 = [], {}, []
+    fs, ft = [], []
+
+    def go_across(c):
+        cross[c] = remote(g.at[0, c, 0:2], g.at[1, c, 0:2], across)
+
     for c in range(NC):
         keep[c].wait()
         sib_g[c].wait_recv()
-        z[0, c] = shift_z(0, c)
-        xc[0, c] = shift_x(0, c, 0, plain1, plain2)
-        cross[c] = remote(g.at[0, c, 0:2], g.at[1, c, 0:2], across)
+        if c in VIA_HIGH:
+            lend(0, c, low)
+    for c in range(NC):
+        to_first(0, c, 0, x >= 1)
+        to_second(0, c, 0, second)
     s0 = spread(lambda yd: g.at[0, :, yd // 2], sl.at[a, y])
     own_s0 = local(g.at[0, :, y // 2], sl.at[a, y])
+    for c in VIA_HIGH:
+        pass_back(0, c)
+        go_across(c)
+    for c in VIA_LOW:
+        shift_z(0, c, low)
+        go_across(c)
+    for c in VIA_HIGH:
+        hand_on(0, c, high)
+    for c in VIA_LOW:
+        to_second(0, c, 0, last)
     sib_of.wait_recv()
-    own_t0, own_s1, own_t1 = [], [], []
-    fs, ft = [], []
-    for c in range(NC):
-        pl.when(wrap2)(z[0, c].wait_recv)
-        shift_x(0, c, 6, wrap1, wrap2)
-        wait_all(xc[0, c])
+
+    def crossed(c):
+        cross[c].wait_recv()
+        to_first(1, c, 0, x >= 1)
+        to_second(1, c, 0, high if c in VIA_LOW else second)
+        if c in VIA_LOW:
+            shift_z(1, c, low)
+        else:
+            lend(1, c, low)
+        s1[c] = spread(lambda yd: g.at[1, c, yd // 2], sb.at[y, c])
+        own_s1[c] = local(g.at[1, c, y // 2], sb.at[y, c])
+
+    for c in range(NC):
+        arrived_first(0, c)
+        seconds[0, c].wait_recv()
         select(0, c)
         t0[c] = spread(lambda yd: tsel.at[0, c, yd], tl.at[a, y, c])
         own_t0.append(local(tsel.at[0, c, y], tl.at[a, y, c]))
-        cross[c].wait_recv()
-        z[1, c] = shift_z(1, c)
-        xc[1, c] = shift_x(1, c, 0, plain1, plain2)
-        s1[c] = spread(lambda yd: g.at[1, c, yd // 2], sb.at[y, c])
-        own_s1.append(local(g.at[1, c, y // 2], sb.at[y, c]))
+        crossed(c)
+        if c >= 1:
+            pass_back(1, c - 1) if c - 1 in VIA_HIGH else None
+        if c >= 2:
+            hand_on(1, c - 2, second)
+    for c in VIA_HIGH:
+        hand_on(1, c, last)
 
     def forward(dst, index):
         return remote(dst.at[a, index], dst.at[a, index], sib)
@@ -182,22 +247,18 @@
             dst[n, c, at1, 0:wide] = -im
             dst[n, c, at1, wide:2 * wide] = re
 
-    tile = 2 * rows
-
     def multiply(left, ch, right, acc, fresh, first, last):
-        def body(i, carry):
-            c = i // 2
-            mt = pl.ds(pl.multiple_of((i % 2) * tile, tile), tile)
-            lh = left[0, ch, mt, :]
+        def body(c, carry):
+            lh = left[0, ch]
             rh = right[0, c]
             r = jnp.dot(lh, rh, preferred_element_type=F32)
             r += jnp.dot(lh, right[1, c], preferred_element_type=F32)
-            r += jnp.dot(left[1, ch, mt, :], rh, preferred_element_type=F32)
+            r += jnp.dot(left[1, ch], rh, preferred_element_type=F32)
             for ri in range(2):
                 v = r[:, ri * wide:(ri + 1) * wide]
-                acc[c, ri, mt, :] = v if fresh else acc[c, ri, mt, :] + v
+                acc[c, ri] = v if fresh else acc[c, ri] + v
             return carry
-        lax.fori_loop(2 * first, 2 * last, body, 0)
+        lax.fori_loop(first, last, body, 0)
 
     def loop(n, fn):
         def body(i, carry):
@@ -213,31 +274,44 @@
         prepare_left(tl, lt, 0, i)
         prepare_left(tl, lt, 1, i)
 
-    for c in range(NC):
-        pl.when(wrap2)(z[1, c].wait_recv)
-        shift_x(1, c, 6, wrap1, wrap2)
-        wait_all(xc[1, c])
+    for cp in own_t0:
+        cp.wait()
+    ft.append(forward(tl, y))
+    for d in (1, 2, 3):
+        for cc in range(NC):
+            t0[cc][d - 1].wait_recv()
+        ft.append(forward(tl, step(y, -d)))
+
+    def prep_left():
+        loop(4, prep_s)
+        loop(4, prep_t)
+        loop(16, lambda i: prepare_right(sl.at[a], rs, i // NC, i % NC))
+        loop(16, lambda i: prepare_right(tl.at[a], rt, i // NC, i % NC))
+
+    wait_all(fs)
+    wait_all(ft)
+
+    for c in VIA_LOW:
+        bring_on(1, c)
+
+    @pl.when(high)
+    def _():
+        prep_left()
+        multiply(ls, h, rt, pacc, True, 0, NC)
+        multiply(lt, h, rs, qacc, True, 0, NC)
+
+    for c in range(NC):
+        arrived_first(1, c)
+        seconds[1, c].wait_recv()
         select(1, c)
         t1[c] = spread(lambda yd: tsel.at[1, c, yd], tb.at[y, c])
         own_t1.append(local(tsel.at[1, c, y], tb.at[y, c]))
-        if c == 0:
-            for cp in own_t0:
-                cp.wait()
-            ft.append(forward(tl, y))
-            for d in (1, 2, 3):
-                for cc in range(NC):
-                    t0[cc][d - 1].wait_recv()
-                ft.append(forward(tl, step(y, -d)))
-            wait_all(fs)
-            loop(4, prep_s)
-            loop(16, lambda i: prepare_right(sl.at[a], rs, i // NC, i % NC))
         if c == 1:
-            wait_all(ft)
-            loop(4, prep_t)
-            loop(16, lambda i: prepare_right(tl.at[a], rt, i // NC, i % NC))
-            multiply(ls, h, rt, pacc, True, 0, NC)
+            pl.when(low)(prep_left)
         if c == 2:
-            multiply(lt, h, rs, qacc, True, 0, NC)
+            pl.when(low)(lambda: multiply(ls, h, rt, pacc, True, 0, NC))
+        if c == 3:
+            pl.when(low)(lambda: multiply(lt, h, rs, qacc, True, 0, NC))
 
     for c in range(NC):
         own_s1[c].wait()
@@ -342,6 +416,7 @@
             pltpu.VMEM((2, 4, 8, 128), F32),
             pltpu.SemaphoreType.DMA((NSEM,)),
             pltpu.SemaphoreType.DMA((NSEM,)),
+            pltpu.SemaphoreType.DMA((NC, 3)),
             pltpu.SemaphoreType.DMA((2, NC, 2)),
             pltpu.SemaphoreType.DMA((2, 2, NC)),
             pltpu.SemaphoreType.DMA((2, 4)),

time: 176 us -> 165 us (0.938)
  Pallas kernels: 171 us -> 159 us
    pallas_call x1, Pallas kernels: 171 us -> 159 us  [body(): pl.pallas_call(functools.partial(kernel, rows), out_shape=(jax.ShapeDtype...]
where the time goes in v3:
time: 165 us
  Pallas kernels  159 us (96%)
  local copies, waits for them, and re-layouts  4.46 us (3%)
    pallas_call x1, Pallas kernels, body(): pl.pallas_call(functools.partial(kernel, rows), out_shape=(jax.ShapeDtype...  159 us

profile of v3, /device:TPU:7, one launch (start us, length us, event | category | flops | bytes accessed | tf_op | source)
XLA Modules:
  0.0 164.5 jit_solution(15977062198036046027)
XLA Ops:
  0.6 159.4 %contract.1 = (f32[2,2,128,1024]{3,2,1,0:T(8,128)}, f32[2,8,128]{2,1,0:T(8,128)}) custom-call(f32[2,128,1024]{2,1,0:T(8,128)} %bitcast.4, s32[1,2]{1,0:T(1,128)} %offs.1), custom_call_target="tpu_custom_call" | custom-call | flops 12999999488 | bytes 4194304 | tf_op jit(solution)/shard_map/contract/pallas_call | solution.py:396
  160.0 1.3 slice_reduce_fusion
  161.4 3.2 %copy.5 = f32[1,2,2,128,1024]{4,3,2,1,0:T(8,128)} copy(f32[1,2,2,128,1024]{4,3,2,1,0:T(8,128)} %bitcast.3) | data formatting | bytes 4194304

commit v4 on v3

--- a/solution.py
+++ b/solution.py
@@ -12,7 +12,7 @@
 BF16 = jnp.bfloat16
 NX, NY, NC = 4, 4, 4
 NSEM = 224
-VIA_HIGH, VIA_LOW = (0, 1), (2, 3)
+VIA_HIGH, VIA_LOW = (0,), (1, 2, 3)
 
 
 def split(value):
@@ -184,9 +184,11 @@
     for c in VIA_HIGH:
         pass_back(0, c)
         go_across(c)
+    go_across(1)
     for c in VIA_LOW:
         shift_z(0, c, low)
-        go_across(c)
+        if c > 1:
+            go_across(c)
     for c in VIA_HIGH:
         hand_on(0, c, high)
     for c in VIA_LOW:
@@ -213,7 +215,7 @@
         crossed(c)
         if c >= 1:
             pass_back(1, c - 1) if c - 1 in VIA_HIGH else None
-        if c >= 2:
+        if c >= 2 and c - 2 in VIA_HIGH:
             hand_on(1, c - 2, second)
     for c in VIA_HIGH:
         hand_on(1, c, last)
@@ -294,7 +296,7 @@
     for c in VIA_LOW:
         bring_on(1, c)
 
-    @pl.when(high)
+    @pl.when(x >= 1)
     def _():
         prep_left()
         multiply(ls, h, rt, pacc, True, 0, NC)
@@ -307,25 +309,27 @@
         t1[c] = spread(lambda yd: tsel.at[1, c, yd], tb.at[y, c])
         own_t1.append(local(tsel.at[1, c, y], tb.at[y, c]))
         if c == 1:
-            pl.when(low)(prep_left)
+            pl.when(x == 0)(prep_left)
         if c == 2:
-            pl.when(low)(lambda: multiply(ls, h, rt, pacc, True, 0, NC))
+            pl.when(x == 0)(lambda: multiply(ls, h, rt, pacc, True, 0, NC))
         if c == 3:
-            pl.when(low)(lambda: multiply(lt, h, rs, qacc, True, 0, NC))
-
-    for c in range(NC):
-        own_s1[c].wait()
-        wait_all(s1[c])
-    loop(16, lambda i: prepare_right(sb, rs, i // NC, i % NC))
-    multiply(lt, 1 - h, rs, qacc, False, 0, NC)
+            pl.when(x == 0)(lambda: multiply(lt, h, rs, qacc, True, 0, NC))
+
+    def cross_rows_of_q():
+        for c in range(NC):
+            own_s1[c].wait()
+            wait_all(s1[c])
+        loop(16, lambda i: prepare_right(sb, rs, i // NC, i % NC))
+        multiply(lt, 1 - h, rs, qacc, False, 0, NC)
 
     src_core = y // 2
     k = y % 2
     home = src_core == a
     away = src_core != a
-    total = jnp.zeros((8, wide), F32)
     back = []
     for c in range(NC):
+        if c == 2:
+            cross_rows_of_q()
         own_t1[c].wait()
         wait_all(t1[c])
         loop(4, lambda i: prepare_right(tb, rt, i, c))
@@ -342,12 +346,16 @@
             else:
                 remote(src, dst, dev(core=src_core, yy=yd), at=psem.at[k, a, c])
 
-        def tr_body(i, acc):
-            at = pl.ds(pl.multiple_of(i * 8, 8), 8)
-            for ri in range(2):
-                acc = acc + pacc[c, ri, at, :] * qacc[c, ri, at, :]
-            return acc
-        total = lax.fori_loop(0, 4 * rows // 8, tr_body, total)
+
+    def tr_body(i, acc):
+        c = i // (4 * rows // 16)
+        at = pl.ds(pl.multiple_of((i % (4 * rows // 16)) * 16, 16), 16)
+        for ri in range(2):
+            v = pacc[c, ri, at, :] * qacc[c, ri, at, :]
+            acc = acc + v
+        return acc
+    total = lax.fori_loop(0, NC * 4 * rows // 16, tr_body, jnp.zeros((16, wide), F32))
+    total = total[0:8] + total[8:16]
 
     part[...] = total
     slot = 2 * h + a
@@ -373,7 +381,7 @@
     width = F32(8 * rows)
     for kk in range(2):
         trace = parts[kk, 0] + parts[kk, 1] + parts[kk, 2] + parts[kk, 3]
-        corr[kk] = jnp.broadcast_to(jnp.sum(trace) / width, corr.shape[1:])
+        corr[0, kk] = jnp.sum(trace) / width
 
     for kk in range(2):
         for ch in range(2):
@@ -395,9 +403,9 @@
     block = (2, rows, 128)
     out, corr = pl.pallas_call(
         functools.partial(kernel, rows),
-        out_shape=(jax.ShapeDtypeStruct((2, 2, rows, width), F32), jax.ShapeDtypeStruct((2, 8, 128), F32)),
+        out_shape=(jax.ShapeDtypeStruct((2, 2, rows, width), F32), jax.ShapeDtypeStruct((1, 2), F32)),
         in_specs=[pl.BlockSpec(memory_space=pl.ANY), pl.BlockSpec(memory_space=pltpu.SMEM)],
-        out_specs=(pl.BlockSpec(memory_space=pl.ANY), pl.BlockSpec(memory_space=pltpu.VMEM)),
+        out_specs=(pl.BlockSpec(memory_space=pl.ANY), pl.BlockSpec(memory_space=pltpu.SMEM)),
         scratch_shapes=[
             pltpu.VMEM((2, NC, 8) + block, F32),
             pltpu.VMEM((2, 2, 8, 128), F32),
@@ -426,7 +434,7 @@
         cost_estimate=pl.CostEstimate(flops=13 * 10**9, bytes_accessed=4 * 2**20, transcendentals=0),
         name="contract",
     )(own, offsets)
-    return out[None], corr[:, 0, 0][None]
+    return out[None], corr
 
 
 def solution(mesh):

time: 165 us -> 163 us (0.988); the launches traced: 165 us -> 161 us
  Pallas kernels: 159 us -> 156 us
    pallas_call x1, Pallas kernels: 159 us -> 156 us  [body(): pl.pallas_call(functools.partial(kernel, rows), out_shape=(jax.ShapeDtype...]
    unnamed x1 -> x4, local copies, waits for them, and re-layouts: 3.16 us -> 3.67 us
where the time goes in v4:
time: 163 us; the launch traced here: 161 us
  Pallas kernels  156 us (96%)
  local copies, waits for them, and re-layouts  3.67 us (2%)
    pallas_call x1, Pallas kernels, body(): pl.pallas_call(functools.partial(kernel, rows), out_shape=(jax.ShapeDtype...  156 us
    unnamed x4, local copies, waits for them, and re-layouts  3.67 us

profile of v4, /device:TPU:7, one launch (start us, length us, event | category | flops | bytes accessed | tf_op | source)
XLA Modules:
  0.0 160.7 jit_solution(14093089556931829371)
XLA Ops:
  0.6 156.3 %contract.1 = (f32[2,2,128,1024]{3,2,1,0:T(8,128)}, f32[1,2]{1,0:T(1,128)}) custom-call(f32[2,128,1024]{2,1,0:T(8,128)} %bitcast.3, s32[1,2]{1,0:T(1,128)} %offs.1), custom_call_target="tpu_custom_call" | custom-call | flops 12999999488 | bytes 4194304 | tf_op jit(solution)/shard_map/contract/pallas_call | solution.py:404
  157.0 0.0 copy-start
  157.0 3.2 %copy.6 = f32[1,2,2,128,1024]{4,3,2,1,0:T(8,128)} copy(f32[1,2,2,128,1024]{4,3,2,1,0:T(8,128)} %bitcast.2) | data formatting | bytes 4194304
  160.1 0.0 copy-done
  160.1 0.5 copy.7
Async XLA Ops:
  157.0 3.2 %copy-start = (f32[1,2]{1,0:T(1,128)S(1)}, f32[1,2]{1,0:T(1,128)}, u32[]{:S(2)}) copy-start(f32[1,2]{1,0:T(1,128)} %get-tuple-element.9) | copy-start | bytes 28
